TPU v7x, 32 devices: a whole 2x2x4 slice. The times are simulated.
32 devices in a mesh: lev: 2 (over x), gx: 8 (over z, y), gy: 2 (over core).
Axes of the slice: x: 2, y: 2, z: 4, core: 2. Of those that a mesh axis runs over, the one named last changes fastest.
Arguments:
- increments: float32 [1, 2, 80, 128, 256], P(None, None, 'lev', 'gx', 'gy'), may hold values from -6 to 6
- vert_corr: float32 [2, 80, 80], replicated, may hold values from -0.025 to 1, as said below
- kappa: float32 [2, 128, 256], P(None, 'gx', 'gy'), may hold values from 0.03 to 0.24
- sea_mask: int32 [80, 128, 256], P('lev', 'gx', 'gy'), may hold values 0 or 1
- level_count: int32 [128, 256], P('gx', 'gy'), may hold values from 10 to 75
Outputs:
- covaried: float32 [1, 2, 80, 128, 256], P(None, None, 'lev', 'gx', 'gy')
Inputs may be any that keep to these rules, and one draw needn't show every extreme that they name: vert_corr has ones on the diagonal, and each row's other entries together have magnitude below one.
All inputs are finite; a program needn't handle non-finite values. No bound on the sum of `sea_mask` on one device may be relied on, other than what follows from the above.
Results may differ from a plain program's by a relative error of at most 0.00021.
Values sent between devices are 32-bit elements; how exact they have to be, the bound alone decides.
A program may use at most 64 MiB of HBM per device.

v0:
```python
import jax
import jax.numpy as jnp
from jax import lax
from jax.sharding import PartitionSpec as P

PASSES = 10


def from_behind(block, axis, distance):
    devices = range(lax.axis_size(axis))
    route = [((i - distance) % len(devices), i) for i in devices]
    return lax.ppermute(block, axis, route)


def shifted(block, axis, distance):
    devices = range(lax.axis_size(axis))
    route = [(i - distance, i) for i in devices if i - distance in devices]
    return lax.ppermute(block, axis, route)


def padded(cells, sides, width):
    for axis, dim in sides:
        count = lax.axis_size(axis)
        head = lax.slice_in_dim(cells, 0, width, axis=dim)
        tail = lax.slice_in_dim(cells, cells.shape[dim] - width, cells.shape[dim], axis=dim)
        cells = jnp.concatenate(
            [
                lax.ppermute(tail, axis, [(i, (i + 1) % count) for i in range(count)]),
                cells,
                lax.ppermute(head, axis, [((i + 1) % count, i) for i in range(count)]),
            ],
            axis=dim,
        )
    return cells


def relax(extended, east_ext, north_ext, wet_center):
    center = extended[..., 1:-1, 1:-1]
    flux = east_ext[1:-1, 1:-1] * (extended[..., 2:, 1:-1] - center)
    flux = flux + east_ext[:-2, 1:-1] * (extended[..., :-2, 1:-1] - center)
    flux = flux + north_ext[1:-1, 1:-1] * (extended[..., 1:-1, 2:] - center)
    flux = flux + north_ext[1:-1, :-2] * (extended[..., 1:-1, :-2] - center)
    return wet_center * (center + flux)


def per_device(increments, vert_corr, kappa, sea_mask, level_count):
    lev_dev = sea_mask.shape[0]
    cells_x = sea_mask.shape[1]
    cells_y = sea_mask.shape[2]
    lev_first = lax.axis_index("lev") * lev_dev
    levels = lev_first + jnp.arange(lev_dev, dtype=jnp.int32)
    wet = sea_mask * (levels[:, None, None] < level_count[None]).astype(jnp.int32)
    wet_float = wet.astype(jnp.float32)
    masked = increments * wet_float
    own_rows = lax.dynamic_slice_in_dim(vert_corr, lev_first, lev_dev, 1)
    correlated = jnp.einsum(
        "toh,dthxy->dtoxy",
        own_rows,
        lax.all_gather(masked, "lev", axis=2, tiled=True),
        precision=lax.Precision.HIGHEST,
    )
    field = correlated * wet_float
    total_y = cells_y * lax.axis_size("gy")
    local_rows = lax.axis_index("gy") * cells_y + jnp.arange(cells_y, dtype=jnp.int32)
    open_local = (local_rows != total_y - 1).astype(jnp.float32)
    east_local = kappa[0]
    north_local = kappa[1] * open_local[None, :]
    east_low = from_behind(east_local[-1:, :], "gx", 1)
    north_low = shifted(north_local[:, -1:], "gy", 1)
    zero_row = jnp.zeros((1, cells_y), jnp.float32)
    zero_col = jnp.zeros((cells_x, 1), jnp.float32)
    east_ext = jnp.pad(jnp.concatenate([east_low, east_local, zero_row], axis=0), ((0, 0), (1, 1)))
    north_ext = jnp.pad(
        jnp.concatenate([north_low, north_local, zero_col], axis=1), ((1, 1), (0, 0))
    )

    def one_pass(step, current):
        extended = padded(current, (("gx", 3), ("gy", 4)), 1)
        return relax(extended, east_ext, north_ext, wet_float)

    field = lax.fori_loop(0, PASSES, one_pass, field)
    return field


def solution(mesh):
    in_specs = (
        P(None, None, "lev", "gx", "gy"),
        P(),
        P(None, "gx", "gy"),
        P("lev", "gx", "gy"),
        P("gx", "gy"),
    )
    out_specs = P(None, None, "lev", "gx", "gy")
    return jax.shard_map(
        per_device, mesh=mesh, in_specs=in_specs, out_specs=out_specs, check_vma=False
    )
```

profile of v0, /device:TPU:0, one launch (start us, length us, event | category | flops | bytes accessed | tf_op | source)
XLA Modules:
  0.0 171.8 jit_solution(11940098655885477659)
XLA Ops:
  7.7 2.1 %copy_multiply_fusion = f32[1,2,40,16,128]{4,2,3,1,0:T(8,128)} fusion(f32[1,2,40,16,128]{4,3,2,1,0:T(8,128)} %param.7, f32[40,16,128]{2,0,1:T(8,128)S(1)} %fusion.21), kind=kLoop, calls=%fused_computation.24 | loop fusion | flops 163840 | bytes 1638400 | tf_op jit(solution)/shard_map/mul | solution.py:54
  9.9 3.0 %collective-permute-start.4 = (f32[1,128]{1,0:T(1,128)S(1)}, f32[1,128]{1,0:T(1,128)S(1)}, u32[]{:S(2)}, u32[]{:S(2)}) collective-permute-start(f32[1,128]{1,0:T(1,128)S(1)} %slice_bitcast_fusion.1), channel_id=1, source_target_pairs={{14,0},{0,2},{2,4},{4,6},{6,8},{8,10},{10,12},{12,14},{15,1},{1,3}... | collective-permute-start | bytes 1544 | tf_op jit(solution)/shard_map/ppermute | solution.py:12
  15.3 2.1 %collective-permute-done.4 = f32[1,128]{1,0:T(1,128)S(1)} collective-permute-done((f32[1,128]{1,0:T(1,128)S(1)}, f32[1,128]{1,0:T(1,128)S(1)}, u32[]{:S(2)}, u32[]{:S(2)}) %collective-permute-start.4) | collective-permute-done | bytes 544 | tf_op jit(solution)/shard_map/ppermute | solution.py:12
  17.6 19.4 %all-gather.2.cloned.1.call-done = f32[1,2,80,16,128]{4,2,3,1,0:T(8,128)} async-done(((f32[1,2,40,16,128]{4,2,3,1,0:T(8,128)}), f32[1,2,80,16,128]{4,2,3,1,0:T(8,128)}) %all-gather.2.cloned.1.call-update) | async-done | bytes 1310736 | tf_op jit(solution)/shard_map/all_gather | solution.py:59
  37.0 3.0 %fusion.18 = f32[1,2,40,16,128]{4,2,3,1,0:T(8,128)} fusion(f32[1,2,80,16,128]{4,2,3,1,0:T(8,128)} %all-gather.2.cloned.1.call-done, f32[40,16,128]{2,0,1:T(8,128)S(1)} %fusion.21, f32[2,80,80]{2,1,0:T(8,128)S(1)} %copy-done, s32[]{:T(128)S(6)} %select_n.3), kind=kOutput, calls=%fused_computation.23 | convolution fusion | flops 157450240 | bytes 2334724 | tf_op jit(solution)/shard_map/toh,dthxy->dtoxy/dot_general | solution.py:56
  40.0 122.9 %while.10 = (s32[]{:T(128)}, f32[1,2,40,16,128]{4,2,3,1,0:T(8,128)}, f32[40,16,128]{2,0,1:T(8,128)S(1)}, f32[18,130]{1,0:T(8,128)S(1)}, f32[18,130]{1,0:T(8,128)S(1)}, /*index=5*/s32[]{:T(128)}) while((s32[]{:T(128)}, f32[1,2,40,16,128]{4,2,3,1,0:T(8,128)}, f32[40,16,128]{2,0,1:T(8,128)S(1)}, f32[18,130]{1,0:T(8,128)S(1)}, ...), condition=%wide.region_1.2_spmd, body=%wide.region_0.1_spmd.sunk | while | flops 2785282 | bytes 5959653 | solution.py:81
  41.1 1.5 collective-permute-start
  42.6 3.2 %collective-permute-start.1 = (f32[1,2,40,1,128]{4,2,3,1,0:T(8,128)S(1)}, f32[1,2,40,1,128]{4,2,3,1,0:T(8,128)S(1)}, u32[]{:S(2)}, u32[]{:S(2)}) collective-permute-start(f32[1,2,40,1,128]{4,2,3,1,0:T(8,128)S(1)} %get-tuple-element.103), channel_id=1, source_target_pairs={{2,0},{4,2},{6,4},{8,6},{10,8},{12,10},{14,12},{0,14},{3,1},{5,3},... | collective-permute-start | bytes 122888 | tf_op jit(solution)/shard_map/while/body/eval_jaxpr/ppermute | solution.py:30
  45.8 2.0 %collective-permute-done = f32[1,2,40,1,128]{4,2,3,1,0:T(8,128)S(1)} collective-permute-done((f32[1,2,40,1,128]{4,2,3,1,0:T(8,128)S(1)}, f32[1,2,40,1,128]{4,2,3,1,0:T(8,128)S(1)}, u32[]{:S(2)}, u32[]{:S(2)}) %collective-permute-start) | collective-permute-done | bytes 40992 | tf_op jit(solution)/shard_map/while/body/eval_jaxpr/ppermute | solution.py:28
  50.8 1.5 fusion.36
  54.5 3.6 %collective-permute-start.1 = (f32[1,2,40,1,128]{4,2,3,1,0:T(8,128)S(1)}, f32[1,2,40,1,128]{4,2,3,1,0:T(8,128)S(1)}, u32[]{:S(2)}, u32[]{:S(2)}) collective-permute-start(f32[1,2,40,1,128]{4,2,3,1,0:T(8,128)S(1)} %get-tuple-element.103), channel_id=1, source_target_pairs={{2,0},{4,2},{6,4},{8,6},{10,8},{12,10},{14,12},{0,14},{3,1},{5,3},... | collective-permute-start | bytes 122888 | tf_op jit(solution)/shard_map/while/body/eval_jaxpr/ppermute | solution.py:30
  58.1 2.0 %collective-permute-done = f32[1,2,40,1,128]{4,2,3,1,0:T(8,128)S(1)} collective-permute-done((f32[1,2,40,1,128]{4,2,3,1,0:T(8,128)S(1)}, f32[1,2,40,1,128]{4,2,3,1,0:T(8,128)S(1)}, u32[]{:S(2)}, u32[]{:S(2)}) %collective-permute-start) | collective-permute-done | bytes 40992 | tf_op jit(solution)/shard_map/while/body/eval_jaxpr/ppermute | solution.py:28
  65.7 4.7 %collective-permute-start.1 = (f32[1,2,40,1,128]{4,2,3,1,0:T(8,128)S(1)}, f32[1,2,40,1,128]{4,2,3,1,0:T(8,128)S(1)}, u32[]{:S(2)}, u32[]{:S(2)}) collective-permute-start(f32[1,2,40,1,128]{4,2,3,1,0:T(8,128)S(1)} %get-tuple-element.103), channel_id=1, source_target_pairs={{2,0},{4,2},{6,4},{8,6},{10,8},{12,10},{14,12},{0,14},{3,1},{5,3},... | collective-permute-start | bytes 122888 | tf_op jit(solution)/shard_map/while/body/eval_jaxpr/ppermute | solution.py:30
  70.4 2.0 %collective-permute-done = f32[1,2,40,1,128]{4,2,3,1,0:T(8,128)S(1)} collective-permute-done((f32[1,2,40,1,128]{4,2,3,1,0:T(8,128)S(1)}, f32[1,2,40,1,128]{4,2,3,1,0:T(8,128)S(1)}, u32[]{:S(2)}, u32[]{:S(2)}) %collective-permute-start) | collective-permute-done | bytes 40992 | tf_op jit(solution)/shard_map/while/body/eval_jaxpr/ppermute | solution.py:28
  77.9 4.7 %collective-permute-start.1 = (f32[1,2,40,1,128]{4,2,3,1,0:T(8,128)S(1)}, f32[1,2,40,1,128]{4,2,3,1,0:T(8,128)S(1)}, u32[]{:S(2)}, u32[]{:S(2)}) collective-permute-start(f32[1,2,40,1,128]{4,2,3,1,0:T(8,128)S(1)} %get-tuple-element.103), channel_id=1, source_target_pairs={{2,0},{4,2},{6,4},{8,6},{10,8},{12,10},{14,12},{0,14},{3,1},{5,3},... | collective-permute-start | bytes 122888 | tf_op jit(solution)/shard_map/while/body/eval_jaxpr/ppermute | solution.py:30
  82.6 2.0 %collective-permute-done = f32[1,2,40,1,128]{4,2,3,1,0:T(8,128)S(1)} collective-permute-done((f32[1,2,40,1,128]{4,2,3,1,0:T(8,128)S(1)}, f32[1,2,40,1,128]{4,2,3,1,0:T(8,128)S(1)}, u32[]{:S(2)}, u32[]{:S(2)}) %collective-permute-start) | collective-permute-done | bytes 40992 | tf_op jit(solution)/shard_map/while/body/eval_jaxpr/ppermute | solution.py:28
  87.7 1.5 fusion.36
  90.2 4.7 %collective-permute-start.1 = (f32[1,2,40,1,128]{4,2,3,1,0:T(8,128)S(1)}, f32[1,2,40,1,128]{4,2,3,1,0:T(8,128)S(1)}, u32[]{:S(2)}, u32[]{:S(2)}) collective-permute-start(f32[1,2,40,1,128]{4,2,3,1,0:T(8,128)S(1)} %get-tuple-element.103), channel_id=1, source_target_pairs={{2,0},{4,2},{6,4},{8,6},{10,8},{12,10},{14,12},{0,14},{3,1},{5,3},... | collective-permute-start | bytes 122888 | tf_op jit(solution)/shard_map/while/body/eval_jaxpr/ppermute | solution.py:30
  95.0 2.0 %collective-permute-done = f32[1,2,40,1,128]{4,2,3,1,0:T(8,128)S(1)} collective-permute-done((f32[1,2,40,1,128]{4,2,3,1,0:T(8,128)S(1)}, f32[1,2,40,1,128]{4,2,3,1,0:T(8,128)S(1)}, u32[]{:S(2)}, u32[]{:S(2)}) %collective-permute-start) | collective-permute-done | bytes 40992 | tf_op jit(solution)/shard_map/while/body/eval_jaxpr/ppermute | solution.py:28
  100.0 1.5 fusion.36
  102.5 4.7 %collective-permute-start.1 = (f32[1,2,40,1,128]{4,2,3,1,0:T(8,128)S(1)}, f32[1,2,40,1,128]{4,2,3,1,0:T(8,128)S(1)}, u32[]{:S(2)}, u32[]{:S(2)}) collective-permute-start(f32[1,2,40,1,128]{4,2,3,1,0:T(8,128)S(1)} %get-tuple-element.103), channel_id=1, source_target_pairs={{2,0},{4,2},{6,4},{8,6},{10,8},{12,10},{14,12},{0,14},{3,1},{5,3},... | collective-permute-start | bytes 122888 | tf_op jit(solution)/shard_map/while/body/eval_jaxpr/ppermute | solution.py:30
  107.2 2.0 %collective-permute-done = f32[1,2,40,1,128]{4,2,3,1,0:T(8,128)S(1)} collective-permute-done((f32[1,2,40,1,128]{4,2,3,1,0:T(8,128)S(1)}, f32[1,2,40,1,128]{4,2,3,1,0:T(8,128)S(1)}, u32[]{:S(2)}, u32[]{:S(2)}) %collective-permute-start) | collective-permute-done | bytes 40992 | tf_op jit(solution)/shard_map/while/body/eval_jaxpr/ppermute | solution.py:28
  114.8 4.7 %collective-permute-start.1 = (f32[1,2,40,1,128]{4,2,3,1,0:T(8,128)S(1)}, f32[1,2,40,1,128]{4,2,3,1,0:T(8,128)S(1)}, u32[]{:S(2)}, u32[]{:S(2)}) collective-permute-start(f32[1,2,40,1,128]{4,2,3,1,0:T(8,128)S(1)} %get-tuple-element.103), channel_id=1, source_target_pairs={{2,0},{4,2},{6,4},{8,6},{10,8},{12,10},{14,12},{0,14},{3,1},{5,3},... | collective-permute-start | bytes 122888 | tf_op jit(solution)/shard_map/while/body/eval_jaxpr/ppermute | solution.py:30
  119.5 2.0 %collective-permute-done = f32[1,2,40,1,128]{4,2,3,1,0:T(8,128)S(1)} collective-permute-done((f32[1,2,40,1,128]{4,2,3,1,0:T(8,128)S(1)}, f32[1,2,40,1,128]{4,2,3,1,0:T(8,128)S(1)}, u32[]{:S(2)}, u32[]{:S(2)}) %collective-permute-start) | collective-permute-done | bytes 40992 | tf_op jit(solution)/shard_map/while/body/eval_jaxpr/ppermute | solution.py:28
  127.1 4.7 %collective-permute-start.1 = (f32[1,2,40,1,128]{4,2,3,1,0:T(8,128)S(1)}, f32[1,2,40,1,128]{4,2,3,1,0:T(8,128)S(1)}, u32[]{:S(2)}, u32[]{:S(2)}) collective-permute-start(f32[1,2,40,1,128]{4,2,3,1,0:T(8,128)S(1)} %get-tuple-element.103), channel_id=1, source_target_pairs={{2,0},{4,2},{6,4},{8,6},{10,8},{12,10},{14,12},{0,14},{3,1},{5,3},... | collective-permute-start | bytes 122888 | tf_op jit(solution)/shard_map/while/body/eval_jaxpr/ppermute | solution.py:30
  131.8 2.0 %collective-permute-done = f32[1,2,40,1,128]{4,2,3,1,0:T(8,128)S(1)} collective-permute-done((f32[1,2,40,1,128]{4,2,3,1,0:T(8,128)S(1)}, f32[1,2,40,1,128]{4,2,3,1,0:T(8,128)S(1)}, u32[]{:S(2)}, u32[]{:S(2)}) %collective-permute-start) | collective-permute-done | bytes 40992 | tf_op jit(solution)/shard_map/while/body/eval_jaxpr/ppermute | solution.py:28
  136.9 1.5 fusion.36
  139.4 4.7 %collective-permute-start.1 = (f32[1,2,40,1,128]{4,2,3,1,0:T(8,128)S(1)}, f32[1,2,40,1,128]{4,2,3,1,0:T(8,128)S(1)}, u32[]{:S(2)}, u32[]{:S(2)}) collective-permute-start(f32[1,2,40,1,128]{4,2,3,1,0:T(8,128)S(1)} %get-tuple-element.103), channel_id=1, source_target_pairs={{2,0},{4,2},{6,4},{8,6},{10,8},{12,10},{14,12},{0,14},{3,1},{5,3},... | collective-permute-start | bytes 122888 | tf_op jit(solution)/shard_map/while/body/eval_jaxpr/ppermute | solution.py:30
  144.1 2.0 %collective-permute-done = f32[1,2,40,1,128]{4,2,3,1,0:T(8,128)S(1)} collective-permute-done((f32[1,2,40,1,128]{4,2,3,1,0:T(8,128)S(1)}, f32[1,2,40,1,128]{4,2,3,1,0:T(8,128)S(1)}, u32[]{:S(2)}, u32[]{:S(2)}) %collective-permute-start) | collective-permute-done | bytes 40992 | tf_op jit(solution)/shard_map/while/body/eval_jaxpr/ppermute | solution.py:28
  151.7 4.7 %collective-permute-start.1 = (f32[1,2,40,1,128]{4,2,3,1,0:T(8,128)S(1)}, f32[1,2,40,1,128]{4,2,3,1,0:T(8,128)S(1)}, u32[]{:S(2)}, u32[]{:S(2)}) collective-permute-start(f32[1,2,40,1,128]{4,2,3,1,0:T(8,128)S(1)} %get-tuple-element.103), channel_id=1, source_target_pairs={{2,0},{4,2},{6,4},{8,6},{10,8},{12,10},{14,12},{0,14},{3,1},{5,3},... | collective-permute-start | bytes 122888 | tf_op jit(solution)/shard_map/while/body/eval_jaxpr/ppermute | solution.py:30
  156.4 2.0 %collective-permute-done = f32[1,2,40,1,128]{4,2,3,1,0:T(8,128)S(1)} collective-permute-done((f32[1,2,40,1,128]{4,2,3,1,0:T(8,128)S(1)}, f32[1,2,40,1,128]{4,2,3,1,0:T(8,128)S(1)}, u32[]{:S(2)}, u32[]{:S(2)}) %collective-permute-start) | collective-permute-done | bytes 40992 | tf_op jit(solution)/shard_map/while/body/eval_jaxpr/ppermute | solution.py:28
  162.9 2.0 %copy.20 = f32[1,2,40,16,128]{4,3,2,1,0:T(8,128)} copy(f32[1,2,40,16,128]{4,2,3,1,0:T(8,128)} %get-tuple-element.32) | data formatting | bytes 1310720 | tf_op jit(solution)/shard_map/while | solution.py:81
  (196 shorter events, 54.5 us)
Async XLA Ops:
  6.5 30.4 %all-gather.2.cloned.1.call-start = ((), (), s32[]{:S(2)}) async-start(), calls=%async_computation | async-start | bytes 1966080 | tf_op jit(solution)/shard_map/all_gather | solution.py:59
  9.9 7.6 %collective-permute-start.4 = (f32[1,128]{1,0:T(1,128)S(1)}, f32[1,128]{1,0:T(1,128)S(1)}, u32[]{:S(2)}, u32[]{:S(2)}) collective-permute-start(f32[1,128]{1,0:T(1,128)S(1)} %slice_bitcast_fusion.1), channel_id=1, source_target_pairs={{14,0},{0,2},{2,4},{4,6},{6,8},{8,10},{10,12},{12,14},{15,1},{1,3}... | collective-permute-start | bytes 1544 | tf_op jit(solution)/shard_map/ppermute | solution.py:12
  13.0 2.3 %collective-permute-start.5 = (f32[16,1]{1,0:T(8,128)S(1)}, f32[16,1]{1,0:T(8,128)S(1)}, u32[]{:S(2)}, u32[]{:S(2)}) collective-permute-start(f32[16,1]{1,0:T(8,128)S(1)} %slice.63), channel_id=1, source_target_pairs={{0,1},{2,3},{4,5},{6,7},{8,9},{10,11},{12,13},{14,15},{16,17},{18,... | collective-permute-start | bytes 200 | tf_op jit(solution)/shard_map/ppermute | solution.py:18
  41.1 6.7 %collective-permute-start = (f32[1,2,40,1,128]{4,2,3,1,0:T(8,128)S(1)}, f32[1,2,40,1,128]{4,2,3,1,0:T(8,128)S(1)}, u32[]{:S(2)}, u32[]{:S(2)}) collective-permute-start(f32[1,2,40,1,128]{4,2,3,1,0:T(8,128)S(1)} %get-tuple-element.102), channel_id=1, source_target_pairs={{0,2},{2,4},{4,6},{6,8},{8,10},{10,12},{12,14},{14,0},{1,3},{3,5},... | collective-permute-start | bytes 122888 | tf_op jit(solution)/shard_map/while/body/eval_jaxpr/ppermute | solution.py:28
  42.6 5.2 %collective-permute-start.1 = (f32[1,2,40,1,128]{4,2,3,1,0:T(8,128)S(1)}, f32[1,2,40,1,128]{4,2,3,1,0:T(8,128)S(1)}, u32[]{:S(2)}, u32[]{:S(2)}) collective-permute-start(f32[1,2,40,1,128]{4,2,3,1,0:T(8,128)S(1)} %get-tuple-element.103), channel_id=1, source_target_pairs={{2,0},{4,2},{6,4},{8,6},{10,8},{12,10},{14,12},{0,14},{3,1},{5,3},... | collective-permute-start | bytes 122888 | tf_op jit(solution)/shard_map/while/body/eval_jaxpr/ppermute | solution.py:30
  48.7 1.8 %collective-permute-start.3 = (f32[1,2,40,18,1]{2,1,4,3,0:T(2,128)S(1)}, f32[1,2,40,18,1]{2,1,4,3,0:T(2,128)S(1)}, u32[]{:S(2)}, u32[]{:S(2)}) collective-permute-start(f32[1,2,40,18,1]{2,1,4,3,0:T(2,128)S(1)} %copy.34), channel_id=1, source_target_pairs={{1,0},{0,1},{3,2},{2,3},{5,4},{4,5},{7,6},{6,7},{9,8},{8,9},{11,10... | collective-permute-start | bytes 17288 | tf_op jit(solution)/shard_map/while/body/eval_jaxpr/ppermute | solution.py:30
  53.3 6.7 %collective-permute-start = (f32[1,2,40,1,128]{4,2,3,1,0:T(8,128)S(1)}, f32[1,2,40,1,128]{4,2,3,1,0:T(8,128)S(1)}, u32[]{:S(2)}, u32[]{:S(2)}) collective-permute-start(f32[1,2,40,1,128]{4,2,3,1,0:T(8,128)S(1)} %get-tuple-element.102), channel_id=1, source_target_pairs={{0,2},{2,4},{4,6},{6,8},{8,10},{10,12},{12,14},{14,0},{1,3},{3,5},... | collective-permute-start | bytes 122888 | tf_op jit(solution)/shard_map/while/body/eval_jaxpr/ppermute | solution.py:28
  54.5 5.7 %collective-permute-start.1 = (f32[1,2,40,1,128]{4,2,3,1,0:T(8,128)S(1)}, f32[1,2,40,1,128]{4,2,3,1,0:T(8,128)S(1)}, u32[]{:S(2)}, u32[]{:S(2)}) collective-permute-start(f32[1,2,40,1,128]{4,2,3,1,0:T(8,128)S(1)} %get-tuple-element.103), channel_id=1, source_target_pairs={{2,0},{4,2},{6,4},{8,6},{10,8},{12,10},{14,12},{0,14},{3,1},{5,3},... | collective-permute-start | bytes 122888 | tf_op jit(solution)/shard_map/while/body/eval_jaxpr/ppermute | solution.py:30
  61.0 1.8 %collective-permute-start.3 = (f32[1,2,40,18,1]{2,1,4,3,0:T(2,128)S(1)}, f32[1,2,40,18,1]{2,1,4,3,0:T(2,128)S(1)}, u32[]{:S(2)}, u32[]{:S(2)}) collective-permute-start(f32[1,2,40,18,1]{2,1,4,3,0:T(2,128)S(1)} %copy.34), channel_id=1, source_target_pairs={{1,0},{0,1},{3,2},{2,3},{5,4},{4,5},{7,6},{6,7},{9,8},{8,9},{11,10... | collective-permute-start | bytes 17288 | tf_op jit(solution)/shard_map/while/body/eval_jaxpr/ppermute | solution.py:30
  65.6 6.7 %collective-permute-start = (f32[1,2,40,1,128]{4,2,3,1,0:T(8,128)S(1)}, f32[1,2,40,1,128]{4,2,3,1,0:T(8,128)S(1)}, u32[]{:S(2)}, u32[]{:S(2)}) collective-permute-start(f32[1,2,40,1,128]{4,2,3,1,0:T(8,128)S(1)} %get-tuple-element.102), channel_id=1, source_target_pairs={{0,2},{2,4},{4,6},{6,8},{8,10},{10,12},{12,14},{14,0},{1,3},{3,5},... | collective-permute-start | bytes 122888 | tf_op jit(solution)/shard_map/while/body/eval_jaxpr/ppermute | solution.py:28
  65.7 6.7 %collective-permute-start.1 = (f32[1,2,40,1,128]{4,2,3,1,0:T(8,128)S(1)}, f32[1,2,40,1,128]{4,2,3,1,0:T(8,128)S(1)}, u32[]{:S(2)}, u32[]{:S(2)}) collective-permute-start(f32[1,2,40,1,128]{4,2,3,1,0:T(8,128)S(1)} %get-tuple-element.103), channel_id=1, source_target_pairs={{2,0},{4,2},{6,4},{8,6},{10,8},{12,10},{14,12},{0,14},{3,1},{5,3},... | collective-permute-start | bytes 122888 | tf_op jit(solution)/shard_map/while/body/eval_jaxpr/ppermute | solution.py:30
  73.3 1.8 %collective-permute-start.3 = (f32[1,2,40,18,1]{2,1,4,3,0:T(2,128)S(1)}, f32[1,2,40,18,1]{2,1,4,3,0:T(2,128)S(1)}, u32[]{:S(2)}, u32[]{:S(2)}) collective-permute-start(f32[1,2,40,18,1]{2,1,4,3,0:T(2,128)S(1)} %copy.34), channel_id=1, source_target_pairs={{1,0},{0,1},{3,2},{2,3},{5,4},{4,5},{7,6},{6,7},{9,8},{8,9},{11,10... | collective-permute-start | bytes 17288 | tf_op jit(solution)/shard_map/while/body/eval_jaxpr/ppermute | solution.py:30
  77.9 6.7 %collective-permute-start = (f32[1,2,40,1,128]{4,2,3,1,0:T(8,128)S(1)}, f32[1,2,40,1,128]{4,2,3,1,0:T(8,128)S(1)}, u32[]{:S(2)}, u32[]{:S(2)}) collective-permute-start(f32[1,2,40,1,128]{4,2,3,1,0:T(8,128)S(1)} %get-tuple-element.102), channel_id=1, source_target_pairs={{0,2},{2,4},{4,6},{6,8},{8,10},{10,12},{12,14},{14,0},{1,3},{3,5},... | collective-permute-start | bytes 122888 | tf_op jit(solution)/shard_map/while/body/eval_jaxpr/ppermute | solution.py:28
  77.9 6.8 %collective-permute-start.1 = (f32[1,2,40,1,128]{4,2,3,1,0:T(8,128)S(1)}, f32[1,2,40,1,128]{4,2,3,1,0:T(8,128)S(1)}, u32[]{:S(2)}, u32[]{:S(2)}) collective-permute-start(f32[1,2,40,1,128]{4,2,3,1,0:T(8,128)S(1)} %get-tuple-element.103), channel_id=1, source_target_pairs={{2,0},{4,2},{6,4},{8,6},{10,8},{12,10},{14,12},{0,14},{3,1},{5,3},... | collective-permute-start | bytes 122888 | tf_op jit(solution)/shard_map/while/body/eval_jaxpr/ppermute | solution.py:30
  85.6 1.8 %collective-permute-start.3 = (f32[1,2,40,18,1]{2,1,4,3,0:T(2,128)S(1)}, f32[1,2,40,18,1]{2,1,4,3,0:T(2,128)S(1)}, u32[]{:S(2)}, u32[]{:S(2)}) collective-permute-start(f32[1,2,40,18,1]{2,1,4,3,0:T(2,128)S(1)} %copy.34), channel_id=1, source_target_pairs={{1,0},{0,1},{3,2},{2,3},{5,4},{4,5},{7,6},{6,7},{9,8},{8,9},{11,10... | collective-permute-start | bytes 17288 | tf_op jit(solution)/shard_map/while/body/eval_jaxpr/ppermute | solution.py:30
  90.2 6.7 %collective-permute-start = (f32[1,2,40,1,128]{4,2,3,1,0:T(8,128)S(1)}, f32[1,2,40,1,128]{4,2,3,1,0:T(8,128)S(1)}, u32[]{:S(2)}, u32[]{:S(2)}) collective-permute-start(f32[1,2,40,1,128]{4,2,3,1,0:T(8,128)S(1)} %get-tuple-element.102), channel_id=1, source_target_pairs={{0,2},{2,4},{4,6},{6,8},{8,10},{10,12},{12,14},{14,0},{1,3},{3,5},... | collective-permute-start | bytes 122888 | tf_op jit(solution)/shard_map/while/body/eval_jaxpr/ppermute | solution.py:28
  90.2 6.7 %collective-permute-start.1 = (f32[1,2,40,1,128]{4,2,3,1,0:T(8,128)S(1)}, f32[1,2,40,1,128]{4,2,3,1,0:T(8,128)S(1)}, u32[]{:S(2)}, u32[]{:S(2)}) collective-permute-start(f32[1,2,40,1,128]{4,2,3,1,0:T(8,128)S(1)} %get-tuple-element.103), channel_id=1, source_target_pairs={{2,0},{4,2},{6,4},{8,6},{10,8},{12,10},{14,12},{0,14},{3,1},{5,3},... | collective-permute-start | bytes 122888 | tf_op jit(solution)/shard_map/while/body/eval_jaxpr/ppermute | solution.py:30
  97.9 1.8 %collective-permute-start.3 = (f32[1,2,40,18,1]{2,1,4,3,0:T(2,128)S(1)}, f32[1,2,40,18,1]{2,1,4,3,0:T(2,128)S(1)}, u32[]{:S(2)}, u32[]{:S(2)}) collective-permute-start(f32[1,2,40,18,1]{2,1,4,3,0:T(2,128)S(1)} %copy.34), channel_id=1, source_target_pairs={{1,0},{0,1},{3,2},{2,3},{5,4},{4,5},{7,6},{6,7},{9,8},{8,9},{11,10... | collective-permute-start | bytes 17288 | tf_op jit(solution)/shard_map/while/body/eval_jaxpr/ppermute | solution.py:30
  102.5 6.7 %collective-permute-start = (f32[1,2,40,1,128]{4,2,3,1,0:T(8,128)S(1)}, f32[1,2,40,1,128]{4,2,3,1,0:T(8,128)S(1)}, u32[]{:S(2)}, u32[]{:S(2)}) collective-permute-start(f32[1,2,40,1,128]{4,2,3,1,0:T(8,128)S(1)} %get-tuple-element.102), channel_id=1, source_target_pairs={{0,2},{2,4},{4,6},{6,8},{8,10},{10,12},{12,14},{14,0},{1,3},{3,5},... | collective-permute-start | bytes 122888 | tf_op jit(solution)/shard_map/while/body/eval_jaxpr/ppermute | solution.py:28
  102.5 6.8 %collective-permute-start.1 = (f32[1,2,40,1,128]{4,2,3,1,0:T(8,128)S(1)}, f32[1,2,40,1,128]{4,2,3,1,0:T(8,128)S(1)}, u32[]{:S(2)}, u32[]{:S(2)}) collective-permute-start(f32[1,2,40,1,128]{4,2,3,1,0:T(8,128)S(1)} %get-tuple-element.103), channel_id=1, source_target_pairs={{2,0},{4,2},{6,4},{8,6},{10,8},{12,10},{14,12},{0,14},{3,1},{5,3},... | collective-permute-start | bytes 122888 | tf_op jit(solution)/shard_map/while/body/eval_jaxpr/ppermute | solution.py:30
  110.2 1.8 %collective-permute-start.3 = (f32[1,2,40,18,1]{2,1,4,3,0:T(2,128)S(1)}, f32[1,2,40,18,1]{2,1,4,3,0:T(2,128)S(1)}, u32[]{:S(2)}, u32[]{:S(2)}) collective-permute-start(f32[1,2,40,18,1]{2,1,4,3,0:T(2,128)S(1)} %copy.34), channel_id=1, source_target_pairs={{1,0},{0,1},{3,2},{2,3},{5,4},{4,5},{7,6},{6,7},{9,8},{8,9},{11,10... | collective-permute-start | bytes 17288 | tf_op jit(solution)/shard_map/while/body/eval_jaxpr/ppermute | solution.py:30
  114.8 6.7 %collective-permute-start = (f32[1,2,40,1,128]{4,2,3,1,0:T(8,128)S(1)}, f32[1,2,40,1,128]{4,2,3,1,0:T(8,128)S(1)}, u32[]{:S(2)}, u32[]{:S(2)}) collective-permute-start(f32[1,2,40,1,128]{4,2,3,1,0:T(8,128)S(1)} %get-tuple-element.102), channel_id=1, source_target_pairs={{0,2},{2,4},{4,6},{6,8},{8,10},{10,12},{12,14},{14,0},{1,3},{3,5},... | collective-permute-start | bytes 122888 | tf_op jit(solution)/shard_map/while/body/eval_jaxpr/ppermute | solution.py:28
  114.8 6.7 %collective-permute-start.1 = (f32[1,2,40,1,128]{4,2,3,1,0:T(8,128)S(1)}, f32[1,2,40,1,128]{4,2,3,1,0:T(8,128)S(1)}, u32[]{:S(2)}, u32[]{:S(2)}) collective-permute-start(f32[1,2,40,1,128]{4,2,3,1,0:T(8,128)S(1)} %get-tuple-element.103), channel_id=1, source_target_pairs={{2,0},{4,2},{6,4},{8,6},{10,8},{12,10},{14,12},{0,14},{3,1},{5,3},... | collective-permute-start | bytes 122888 | tf_op jit(solution)/shard_map/while/body/eval_jaxpr/ppermute | solution.py:30
  122.5 1.8 %collective-permute-start.3 = (f32[1,2,40,18,1]{2,1,4,3,0:T(2,128)S(1)}, f32[1,2,40,18,1]{2,1,4,3,0:T(2,128)S(1)}, u32[]{:S(2)}, u32[]{:S(2)}) collective-permute-start(f32[1,2,40,18,1]{2,1,4,3,0:T(2,128)S(1)} %copy.34), channel_id=1, source_target_pairs={{1,0},{0,1},{3,2},{2,3},{5,4},{4,5},{7,6},{6,7},{9,8},{8,9},{11,10... | collective-permute-start | bytes 17288 | tf_op jit(solution)/shard_map/while/body/eval_jaxpr/ppermute | solution.py:30
  127.1 6.7 %collective-permute-start = (f32[1,2,40,1,128]{4,2,3,1,0:T(8,128)S(1)}, f32[1,2,40,1,128]{4,2,3,1,0:T(8,128)S(1)}, u32[]{:S(2)}, u32[]{:S(2)}) collective-permute-start(f32[1,2,40,1,128]{4,2,3,1,0:T(8,128)S(1)} %get-tuple-element.102), channel_id=1, source_target_pairs={{0,2},{2,4},{4,6},{6,8},{8,10},{10,12},{12,14},{14,0},{1,3},{3,5},... | collective-permute-start | bytes 122888 | tf_op jit(solution)/shard_map/while/body/eval_jaxpr/ppermute | solution.py:28
  127.1 6.8 %collective-permute-start.1 = (f32[1,2,40,1,128]{4,2,3,1,0:T(8,128)S(1)}, f32[1,2,40,1,128]{4,2,3,1,0:T(8,128)S(1)}, u32[]{:S(2)}, u32[]{:S(2)}) collective-permute-start(f32[1,2,40,1,128]{4,2,3,1,0:T(8,128)S(1)} %get-tuple-element.103), channel_id=1, source_target_pairs={{2,0},{4,2},{6,4},{8,6},{10,8},{12,10},{14,12},{0,14},{3,1},{5,3},... | collective-permute-start | bytes 122888 | tf_op jit(solution)/shard_map/while/body/eval_jaxpr/ppermute | solution.py:30
  134.8 1.8 %collective-permute-start.3 = (f32[1,2,40,18,1]{2,1,4,3,0:T(2,128)S(1)}, f32[1,2,40,18,1]{2,1,4,3,0:T(2,128)S(1)}, u32[]{:S(2)}, u32[]{:S(2)}) collective-permute-start(f32[1,2,40,18,1]{2,1,4,3,0:T(2,128)S(1)} %copy.34), channel_id=1, source_target_pairs={{1,0},{0,1},{3,2},{2,3},{5,4},{4,5},{7,6},{6,7},{9,8},{8,9},{11,10... | collective-permute-start | bytes 17288 | tf_op jit(solution)/shard_map/while/body/eval_jaxpr/ppermute | solution.py:30
  139.4 6.7 %collective-permute-start = (f32[1,2,40,1,128]{4,2,3,1,0:T(8,128)S(1)}, f32[1,2,40,1,128]{4,2,3,1,0:T(8,128)S(1)}, u32[]{:S(2)}, u32[]{:S(2)}) collective-permute-start(f32[1,2,40,1,128]{4,2,3,1,0:T(8,128)S(1)} %get-tuple-element.102), channel_id=1, source_target_pairs={{0,2},{2,4},{4,6},{6,8},{8,10},{10,12},{12,14},{14,0},{1,3},{3,5},... | collective-permute-start | bytes 122888 | tf_op jit(solution)/shard_map/while/body/eval_jaxpr/ppermute | solution.py:28
  139.4 6.7 %collective-permute-start.1 = (f32[1,2,40,1,128]{4,2,3,1,0:T(8,128)S(1)}, f32[1,2,40,1,128]{4,2,3,1,0:T(8,128)S(1)}, u32[]{:S(2)}, u32[]{:S(2)}) collective-permute-start(f32[1,2,40,1,128]{4,2,3,1,0:T(8,128)S(1)} %get-tuple-element.103), channel_id=1, source_target_pairs={{2,0},{4,2},{6,4},{8,6},{10,8},{12,10},{14,12},{0,14},{3,1},{5,3},... | collective-permute-start | bytes 122888 | tf_op jit(solution)/shard_map/while/body/eval_jaxpr/ppermute | solution.py:30
  147.0 1.8 %collective-permute-start.3 = (f32[1,2,40,18,1]{2,1,4,3,0:T(2,128)S(1)}, f32[1,2,40,18,1]{2,1,4,3,0:T(2,128)S(1)}, u32[]{:S(2)}, u32[]{:S(2)}) collective-permute-start(f32[1,2,40,18,1]{2,1,4,3,0:T(2,128)S(1)} %copy.34), channel_id=1, source_target_pairs={{1,0},{0,1},{3,2},{2,3},{5,4},{4,5},{7,6},{6,7},{9,8},{8,9},{11,10... | collective-permute-start | bytes 17288 | tf_op jit(solution)/shard_map/while/body/eval_jaxpr/ppermute | solution.py:30
  151.7 6.7 %collective-permute-start = (f32[1,2,40,1,128]{4,2,3,1,0:T(8,128)S(1)}, f32[1,2,40,1,128]{4,2,3,1,0:T(8,128)S(1)}, u32[]{:S(2)}, u32[]{:S(2)}) collective-permute-start(f32[1,2,40,1,128]{4,2,3,1,0:T(8,128)S(1)} %get-tuple-element.102), channel_id=1, source_target_pairs={{0,2},{2,4},{4,6},{6,8},{8,10},{10,12},{12,14},{14,0},{1,3},{3,5},... | collective-permute-start | bytes 122888 | tf_op jit(solution)/shard_map/while/body/eval_jaxpr/ppermute | solution.py:28
  151.7 6.8 %collective-permute-start.1 = (f32[1,2,40,1,128]{4,2,3,1,0:T(8,128)S(1)}, f32[1,2,40,1,128]{4,2,3,1,0:T(8,128)S(1)}, u32[]{:S(2)}, u32[]{:S(2)}) collective-permute-start(f32[1,2,40,1,128]{4,2,3,1,0:T(8,128)S(1)} %get-tuple-element.103), channel_id=1, source_target_pairs={{2,0},{4,2},{6,4},{8,6},{10,8},{12,10},{14,12},{0,14},{3,1},{5,3},... | collective-permute-start | bytes 122888 | tf_op jit(solution)/shard_map/while/body/eval_jaxpr/ppermute | solution.py:30
  (13 other events, 47.7 us)
Sparse Core Ops, SparseCore 0:
  10.0 26.9 all-gather.1
where the time goes:
time: 172 us
  starting transfers between devices  57.3 us (33%)
  waiting for transfers between devices  49.7 us (29%)
  local copies, waits for them, and re-layouts  29.9 us (17%)
  other arithmetic  17.9 us (10%)
  between operations  13.4 us (8%)
  matrix products  3.01 us (2%)
    ppermute x20, starting transfers between devices, padded(): lax.ppermute(head, axis, [((i + 1) % count, i) for i in range(count)])  45.2 us
    ppermute x20, waiting for transfers between devices, padded(): lax.ppermute(tail, axis, [(i, (i + 1) % count) for i in range(count)])  27.5 us
    all_gather x1, waiting for transfers between devices, per_device(): lax.all_gather(masked, 'lev', axis=2, tiled=True)  19.4 us
    while x50, local copies, waits for them, and re-layouts  17.4 us
    mul x10, other arithmetic, relax(): return wet_center * (center + flux)  14.5 us
    ppermute x20, starting transfers between devices, padded(): lax.ppermute(tail, axis, [(i, (i + 1) % count) for i in range(count)])  7.65 us
  transfers between devices with their start and end apart: 43, of which 23 were waited for; matrix products, arithmetic and copies ran while one was open for 3% of the time, Pallas kernels for 0%

commit v1 on v0

--- a/solution.py
+++ b/solution.py
@@ -44,6 +44,20 @@
 
 
 def per_device(increments, vert_corr, kappa, sea_mask, level_count):
+
+    def track_gates(field_in, target):
+        block_list = []
+        x_next, arr_next = (lax.psum(1, axis_name="lev"), lax.axis_index("lev"))
+        for dev_j in range(x_next):
+            block_list.append((dev_j, (dev_j - 1) % x_next))
+        all_rows = field_in
+        tile_out = field_in.shape[2]
+        b_next = target(all_rows, arr_next * tile_out)
+        for hop_no in range(1, x_next):
+            all_rows = lax.ppermute(all_rows, axis_name="lev", perm=block_list)
+            b_next = b_next + target(all_rows, (arr_next + hop_no) % x_next * tile_out)
+        return b_next
+
     lev_dev = sea_mask.shape[0]
     cells_x = sea_mask.shape[1]
     cells_y = sea_mask.shape[2]
@@ -53,11 +67,14 @@
     wet_float = wet.astype(jnp.float32)
     masked = increments * wet_float
     own_rows = lax.dynamic_slice_in_dim(vert_corr, lev_first, lev_dev, 1)
-    correlated = jnp.einsum(
-        "toh,dthxy->dtoxy",
-        own_rows,
-        lax.all_gather(masked, "lev", axis=2, tiled=True),
-        precision=lax.Precision.HIGHEST,
+    correlated = track_gates(
+        masked,
+        lambda own_block, offset: jnp.einsum(
+            "toh,dthxy->dtoxy",
+            lax.dynamic_slice_in_dim(own_rows, offset, own_block.shape[2], axis=2),
+            own_block,
+            precision=lax.Precision.HIGHEST,
+        ),
     )
     field = correlated * wet_float
     total_y = cells_y * lax.axis_size("gy")

time: 172 us -> 151 us (0.88)
  between operations: 13.4 us -> 0.1 us
  waiting for transfers between devices: 49.7 us -> 41 us
    all_gather x1 -> x0, waiting for transfers between devices: 19.4 us -> none  [per_device(): lax.all_gather(masked, 'lev', axis=2, tiled=True)]
    ppermute x0 -> x1, waiting for transfers between devices: none -> 13.4 us  [track_gates(): all_rows = lax.ppermute(all_rows, axis_name='lev', perm=block_list)]
    ppermute x1, waiting for transfers between devices: 2.12 us -> 0.01 us  [from_behind(): return lax.ppermute(block, axis, route)]
    mul x1, other arithmetic: 2.14 us -> 0.21 us  [per_device(): masked = increments * wet_float]
  transfers between devices with their start and end apart: 43 -> 43, of which waited for: 23 -> 21; matrix products, arithmetic and copies ran while one was open for 3% -> 5% of each run, Pallas kernels for 0% -> 0%
where the time goes in v1:
time: 151 us; the launch traced here: 150 us
  starting transfers between devices  58.8 us (39%)
  waiting for transfers between devices  41 us (27%)
  local copies, waits for them, and re-layouts  30.6 us (20%)
  other arithmetic  16.6 us (11%)
  matrix products  2.3 us (2%)
    ppermute x20, starting transfers between devices, padded(): lax.ppermute(head, axis, [((i + 1) % count, i) for i in range(count)])  45.2 us
    ppermute x20, waiting for transfers between devices, padded(): lax.ppermute(tail, axis, [(i, (i + 1) % count) for i in range(count)])  27.5 us
    while x50, local copies, waits for them, and re-layouts  17.4 us
    mul x10, other arithmetic, relax(): return wet_center * (center + flux)  14.4 us
    ppermute x1, waiting for transfers between devices, track_gates(): all_rows = lax.ppermute(all_rows, axis_name='lev', perm=block_list)  13.4 us
    ppermute x20, starting transfers between devices, padded(): lax.ppermute(tail, axis, [(i, (i + 1) % count) for i in range(count)])  7.68 us
    ppermute x10, local copies, waits for them, and re-layouts, padded(): lax.ppermute(head, axis, [((i + 1) % count, i) for i in range(count)])  3.31 us
    ppermute x10, local copies, waits for them, and re-layouts, padded(): lax.ppermute(tail, axis, [(i, (i + 1) % count) for i in range(count)])  3.3 us
  transfers between devices with their start and end apart: 43, of which 21 were waited for; matrix products, arithmetic and copies ran while one was open for 5% of the time, Pallas kernels for 0%

profile of v1, /device:TPU:0, one launch (start us, length us, event | category | flops | bytes accessed | tf_op | source)
XLA Modules:
  0.0 149.9 jit_solution(1145603845038606674)
XLA Ops:
  0.8 3.0 %collective-permute-start.5 = (f32[1,128]{1,0:T(1,128)S(1)}, f32[1,128]{1,0:T(1,128)S(1)}, u32[]{:S(2)}, u32[]{:S(2)}) collective-permute-start(f32[1,128]{1,0:T(1,128)S(1)} %slice_bitcast_fusion.1), channel_id=1, source_target_pairs={{14,0},{0,2},{2,4},{4,6},{6,8},{8,10},{10,12},{12,14},{15,1},{1,3}... | collective-permute-start | bytes 1544 | tf_op jit(solution)/shard_map/ppermute | solution.py:12
  4.5 1.4 collective-permute-start.6
  7.3 1.6 %collective-permute-start.4 = (f32[1,2,40,16,128]{4,2,3,1,0:T(8,128)S(1)}, f32[1,2,40,16,128]{4,2,3,1,0:T(8,128)S(1)}, u32[]{:S(2)}, u32[]{:S(2)}) collective-permute-start(f32[1,2,40,16,128]{4,2,3,1,0:T(8,128)S(1)} %copy_multiply_fusion), channel_id=1, source_target_pairs={{0,16},{16,0},{1,17},{17,1},{2,18},{18,2},{3,19},{19,3},{4,20},{20... | collective-permute-start | bytes 1966088 | tf_op jit(solution)/shard_map/ppermute | solution.py:57
  10.0 13.4 %collective-permute-done.4 = f32[1,2,40,16,128]{4,2,3,1,0:T(8,128)S(1)} collective-permute-done((f32[1,2,40,16,128]{4,2,3,1,0:T(8,128)S(1)}, f32[1,2,40,16,128]{4,2,3,1,0:T(8,128)S(1)}, u32[]{:S(2)}, u32[]{:S(2)}) %collective-permute-start.4) | collective-permute-done | bytes 655392 | tf_op jit(solution)/shard_map/ppermute | solution.py:57
  23.4 1.6 %fusion.14 = f32[1,2,40,16,128]{4,2,3,1,0:T(8,128)} fusion(f32[2,16,128,40]{2,3,1,0:T(8,128)S(1)} %fusion.16, f32[1,2,40,16,128]{4,2,3,1,0:T(8,128)S(1)} %collective-permute-done.4, f32[40,16,128]{2,0,1:T(8,128)S(1)} %fusion.18, f32[2,80,80]{2,1,0:T(8,128)S(1)} %copy-done, s32[]{:T(128)S(6)} %select_n.19, s32[]{:T(128)S(6)} %select_n.22), kind=kOutput, calls=%fused_computation.22 | convolution fusion | flops 78970880 | bytes 2334728 | tf_op jit(solution)/shard_map/toh,dthxy->dtoxy/dot_general | solution.py:72
  25.0 122.9 %while.10 = (s32[]{:T(128)}, f32[1,2,40,16,128]{4,2,3,1,0:T(8,128)}, f32[40,16,128]{2,0,1:T(8,128)S(1)}, f32[18,130]{1,0:T(8,128)S(1)}, f32[18,130]{1,0:T(8,128)S(1)}, /*index=5*/s32[]{:T(128)}) while((s32[]{:T(128)}, f32[1,2,40,16,128]{4,2,3,1,0:T(8,128)}, f32[40,16,128]{2,0,1:T(8,128)S(1)}, f32[18,130]{1,0:T(8,128)S(1)}, ...), condition=%wide.region_1.2_spmd, body=%wide.region_0.1_spmd.sunk | while | flops 2785282 | bytes 5959653 | solution.py:98
  26.1 1.5 %collective-permute-start = (f32[1,2,40,1,128]{4,2,3,1,0:T(8,128)S(1)}, f32[1,2,40,1,128]{4,2,3,1,0:T(8,128)S(1)}, u32[]{:S(2)}, u32[]{:S(2)}) collective-permute-start(f32[1,2,40,1,128]{4,2,3,1,0:T(8,128)S(1)} %get-tuple-element.102), channel_id=1, source_target_pairs={{0,2},{2,4},{4,6},{6,8},{8,10},{10,12},{12,14},{14,0},{1,3},{3,5},... | collective-permute-start | bytes 122888 | tf_op jit(solution)/shard_map/while/body/eval_jaxpr/ppermute | solution.py:28
  27.6 3.2 %collective-permute-start.1 = (f32[1,2,40,1,128]{4,2,3,1,0:T(8,128)S(1)}, f32[1,2,40,1,128]{4,2,3,1,0:T(8,128)S(1)}, u32[]{:S(2)}, u32[]{:S(2)}) collective-permute-start(f32[1,2,40,1,128]{4,2,3,1,0:T(8,128)S(1)} %get-tuple-element.103), channel_id=1, source_target_pairs={{2,0},{4,2},{6,4},{8,6},{10,8},{12,10},{14,12},{0,14},{3,1},{5,3},... | collective-permute-start | bytes 122888 | tf_op jit(solution)/shard_map/while/body/eval_jaxpr/ppermute | solution.py:30
  30.8 2.0 %collective-permute-done = f32[1,2,40,1,128]{4,2,3,1,0:T(8,128)S(1)} collective-permute-done((f32[1,2,40,1,128]{4,2,3,1,0:T(8,128)S(1)}, f32[1,2,40,1,128]{4,2,3,1,0:T(8,128)S(1)}, u32[]{:S(2)}, u32[]{:S(2)}) %collective-permute-start) | collective-permute-done | bytes 40992 | tf_op jit(solution)/shard_map/while/body/eval_jaxpr/ppermute | solution.py:28
  35.8 1.4 fusion.36
  39.5 3.6 %collective-permute-start.1 = (f32[1,2,40,1,128]{4,2,3,1,0:T(8,128)S(1)}, f32[1,2,40,1,128]{4,2,3,1,0:T(8,128)S(1)}, u32[]{:S(2)}, u32[]{:S(2)}) collective-permute-start(f32[1,2,40,1,128]{4,2,3,1,0:T(8,128)S(1)} %get-tuple-element.103), channel_id=1, source_target_pairs={{2,0},{4,2},{6,4},{8,6},{10,8},{12,10},{14,12},{0,14},{3,1},{5,3},... | collective-permute-start | bytes 122888 | tf_op jit(solution)/shard_map/while/body/eval_jaxpr/ppermute | solution.py:30
  43.1 2.0 %collective-permute-done = f32[1,2,40,1,128]{4,2,3,1,0:T(8,128)S(1)} collective-permute-done((f32[1,2,40,1,128]{4,2,3,1,0:T(8,128)S(1)}, f32[1,2,40,1,128]{4,2,3,1,0:T(8,128)S(1)}, u32[]{:S(2)}, u32[]{:S(2)}) %collective-permute-start) | collective-permute-done | bytes 40992 | tf_op jit(solution)/shard_map/while/body/eval_jaxpr/ppermute | solution.py:28
  48.1 1.4 fusion.36
  50.7 4.7 %collective-permute-start.1 = (f32[1,2,40,1,128]{4,2,3,1,0:T(8,128)S(1)}, f32[1,2,40,1,128]{4,2,3,1,0:T(8,128)S(1)}, u32[]{:S(2)}, u32[]{:S(2)}) collective-permute-start(f32[1,2,40,1,128]{4,2,3,1,0:T(8,128)S(1)} %get-tuple-element.103), channel_id=1, source_target_pairs={{2,0},{4,2},{6,4},{8,6},{10,8},{12,10},{14,12},{0,14},{3,1},{5,3},... | collective-permute-start | bytes 122888 | tf_op jit(solution)/shard_map/while/body/eval_jaxpr/ppermute | solution.py:30
  55.4 2.0 %collective-permute-done = f32[1,2,40,1,128]{4,2,3,1,0:T(8,128)S(1)} collective-permute-done((f32[1,2,40,1,128]{4,2,3,1,0:T(8,128)S(1)}, f32[1,2,40,1,128]{4,2,3,1,0:T(8,128)S(1)}, u32[]{:S(2)}, u32[]{:S(2)}) %collective-permute-start) | collective-permute-done | bytes 40992 | tf_op jit(solution)/shard_map/while/body/eval_jaxpr/ppermute | solution.py:28
  60.4 1.4 fusion.36
  62.9 4.7 %collective-permute-start.1 = (f32[1,2,40,1,128]{4,2,3,1,0:T(8,128)S(1)}, f32[1,2,40,1,128]{4,2,3,1,0:T(8,128)S(1)}, u32[]{:S(2)}, u32[]{:S(2)}) collective-permute-start(f32[1,2,40,1,128]{4,2,3,1,0:T(8,128)S(1)} %get-tuple-element.103), channel_id=1, source_target_pairs={{2,0},{4,2},{6,4},{8,6},{10,8},{12,10},{14,12},{0,14},{3,1},{5,3},... | collective-permute-start | bytes 122888 | tf_op jit(solution)/shard_map/while/body/eval_jaxpr/ppermute | solution.py:30
  67.6 2.0 %collective-permute-done = f32[1,2,40,1,128]{4,2,3,1,0:T(8,128)S(1)} collective-permute-done((f32[1,2,40,1,128]{4,2,3,1,0:T(8,128)S(1)}, f32[1,2,40,1,128]{4,2,3,1,0:T(8,128)S(1)}, u32[]{:S(2)}, u32[]{:S(2)}) %collective-permute-start) | collective-permute-done | bytes 40992 | tf_op jit(solution)/shard_map/while/body/eval_jaxpr/ppermute | solution.py:28
  72.7 1.4 fusion.36
  75.2 4.7 %collective-permute-start.1 = (f32[1,2,40,1,128]{4,2,3,1,0:T(8,128)S(1)}, f32[1,2,40,1,128]{4,2,3,1,0:T(8,128)S(1)}, u32[]{:S(2)}, u32[]{:S(2)}) collective-permute-start(f32[1,2,40,1,128]{4,2,3,1,0:T(8,128)S(1)} %get-tuple-element.103), channel_id=1, source_target_pairs={{2,0},{4,2},{6,4},{8,6},{10,8},{12,10},{14,12},{0,14},{3,1},{5,3},... | collective-permute-start | bytes 122888 | tf_op jit(solution)/shard_map/while/body/eval_jaxpr/ppermute | solution.py:30
  79.9 2.0 %collective-permute-done = f32[1,2,40,1,128]{4,2,3,1,0:T(8,128)S(1)} collective-permute-done((f32[1,2,40,1,128]{4,2,3,1,0:T(8,128)S(1)}, f32[1,2,40,1,128]{4,2,3,1,0:T(8,128)S(1)}, u32[]{:S(2)}, u32[]{:S(2)}) %collective-permute-start) | collective-permute-done | bytes 40992 | tf_op jit(solution)/shard_map/while/body/eval_jaxpr/ppermute | solution.py:28
  87.5 4.7 %collective-permute-start.1 = (f32[1,2,40,1,128]{4,2,3,1,0:T(8,128)S(1)}, f32[1,2,40,1,128]{4,2,3,1,0:T(8,128)S(1)}, u32[]{:S(2)}, u32[]{:S(2)}) collective-permute-start(f32[1,2,40,1,128]{4,2,3,1,0:T(8,128)S(1)} %get-tuple-element.103), channel_id=1, source_target_pairs={{2,0},{4,2},{6,4},{8,6},{10,8},{12,10},{14,12},{0,14},{3,1},{5,3},... | collective-permute-start | bytes 122888 | tf_op jit(solution)/shard_map/while/body/eval_jaxpr/ppermute | solution.py:30
  92.2 2.0 %collective-permute-done = f32[1,2,40,1,128]{4,2,3,1,0:T(8,128)S(1)} collective-permute-done((f32[1,2,40,1,128]{4,2,3,1,0:T(8,128)S(1)}, f32[1,2,40,1,128]{4,2,3,1,0:T(8,128)S(1)}, u32[]{:S(2)}, u32[]{:S(2)}) %collective-permute-start) | collective-permute-done | bytes 40992 | tf_op jit(solution)/shard_map/while/body/eval_jaxpr/ppermute | solution.py:28
  99.8 4.7 %collective-permute-start.1 = (f32[1,2,40,1,128]{4,2,3,1,0:T(8,128)S(1)}, f32[1,2,40,1,128]{4,2,3,1,0:T(8,128)S(1)}, u32[]{:S(2)}, u32[]{:S(2)}) collective-permute-start(f32[1,2,40,1,128]{4,2,3,1,0:T(8,128)S(1)} %get-tuple-element.103), channel_id=1, source_target_pairs={{2,0},{4,2},{6,4},{8,6},{10,8},{12,10},{14,12},{0,14},{3,1},{5,3},... | collective-permute-start | bytes 122888 | tf_op jit(solution)/shard_map/while/body/eval_jaxpr/ppermute | solution.py:30
  104.5 2.0 %collective-permute-done = f32[1,2,40,1,128]{4,2,3,1,0:T(8,128)S(1)} collective-permute-done((f32[1,2,40,1,128]{4,2,3,1,0:T(8,128)S(1)}, f32[1,2,40,1,128]{4,2,3,1,0:T(8,128)S(1)}, u32[]{:S(2)}, u32[]{:S(2)}) %collective-permute-start) | collective-permute-done | bytes 40992 | tf_op jit(solution)/shard_map/while/body/eval_jaxpr/ppermute | solution.py:28
  112.1 4.7 %collective-permute-start.1 = (f32[1,2,40,1,128]{4,2,3,1,0:T(8,128)S(1)}, f32[1,2,40,1,128]{4,2,3,1,0:T(8,128)S(1)}, u32[]{:S(2)}, u32[]{:S(2)}) collective-permute-start(f32[1,2,40,1,128]{4,2,3,1,0:T(8,128)S(1)} %get-tuple-element.103), channel_id=1, source_target_pairs={{2,0},{4,2},{6,4},{8,6},{10,8},{12,10},{14,12},{0,14},{3,1},{5,3},... | collective-permute-start | bytes 122888 | tf_op jit(solution)/shard_map/while/body/eval_jaxpr/ppermute | solution.py:30
  116.8 2.0 %collective-permute-done = f32[1,2,40,1,128]{4,2,3,1,0:T(8,128)S(1)} collective-permute-done((f32[1,2,40,1,128]{4,2,3,1,0:T(8,128)S(1)}, f32[1,2,40,1,128]{4,2,3,1,0:T(8,128)S(1)}, u32[]{:S(2)}, u32[]{:S(2)}) %collective-permute-start) | collective-permute-done | bytes 40992 | tf_op jit(solution)/shard_map/while/body/eval_jaxpr/ppermute | solution.py:28
  124.4 4.7 %collective-permute-start.1 = (f32[1,2,40,1,128]{4,2,3,1,0:T(8,128)S(1)}, f32[1,2,40,1,128]{4,2,3,1,0:T(8,128)S(1)}, u32[]{:S(2)}, u32[]{:S(2)}) collective-permute-start(f32[1,2,40,1,128]{4,2,3,1,0:T(8,128)S(1)} %get-tuple-element.103), channel_id=1, source_target_pairs={{2,0},{4,2},{6,4},{8,6},{10,8},{12,10},{14,12},{0,14},{3,1},{5,3},... | collective-permute-start | bytes 122888 | tf_op jit(solution)/shard_map/while/body/eval_jaxpr/ppermute | solution.py:30
  129.1 2.0 %collective-permute-done = f32[1,2,40,1,128]{4,2,3,1,0:T(8,128)S(1)} collective-permute-done((f32[1,2,40,1,128]{4,2,3,1,0:T(8,128)S(1)}, f32[1,2,40,1,128]{4,2,3,1,0:T(8,128)S(1)}, u32[]{:S(2)}, u32[]{:S(2)}) %collective-permute-start) | collective-permute-done | bytes 40992 | tf_op jit(solution)/shard_map/while/body/eval_jaxpr/ppermute | solution.py:28
  136.7 4.7 %collective-permute-start.1 = (f32[1,2,40,1,128]{4,2,3,1,0:T(8,128)S(1)}, f32[1,2,40,1,128]{4,2,3,1,0:T(8,128)S(1)}, u32[]{:S(2)}, u32[]{:S(2)}) collective-permute-start(f32[1,2,40,1,128]{4,2,3,1,0:T(8,128)S(1)} %get-tuple-element.103), channel_id=1, source_target_pairs={{2,0},{4,2},{6,4},{8,6},{10,8},{12,10},{14,12},{0,14},{3,1},{5,3},... | collective-permute-start | bytes 122888 | tf_op jit(solution)/shard_map/while/body/eval_jaxpr/ppermute | solution.py:30
  141.4 2.0 %collective-permute-done = f32[1,2,40,1,128]{4,2,3,1,0:T(8,128)S(1)} collective-permute-done((f32[1,2,40,1,128]{4,2,3,1,0:T(8,128)S(1)}, f32[1,2,40,1,128]{4,2,3,1,0:T(8,128)S(1)}, u32[]{:S(2)}, u32[]{:S(2)}) %collective-permute-start) | collective-permute-done | bytes 40992 | tf_op jit(solution)/shard_map/while/body/eval_jaxpr/ppermute | solution.py:28
  147.8 2.0 %copy.20 = f32[1,2,40,16,128]{4,3,2,1,0:T(8,128)} copy(f32[1,2,40,16,128]{4,2,3,1,0:T(8,128)} %get-tuple-element.32) | data formatting | bytes 1310720 | tf_op jit(solution)/shard_map/while | solution.py:98
  (198 shorter events, 54.7 us)
Async XLA Ops:
  0.8 9.1 %collective-permute-start.5 = (f32[1,128]{1,0:T(1,128)S(1)}, f32[1,128]{1,0:T(1,128)S(1)}, u32[]{:S(2)}, u32[]{:S(2)}) collective-permute-start(f32[1,128]{1,0:T(1,128)S(1)} %slice_bitcast_fusion.1), channel_id=1, source_target_pairs={{14,0},{0,2},{2,4},{4,6},{6,8},{8,10},{10,12},{12,14},{15,1},{1,3}... | collective-permute-start | bytes 1544 | tf_op jit(solution)/shard_map/ppermute | solution.py:12
  4.5 5.3 %collective-permute-start.6 = (f32[16,1]{1,0:T(8,128)S(1)}, f32[16,1]{1,0:T(8,128)S(1)}, u32[]{:S(2)}, u32[]{:S(2)}) collective-permute-start(f32[16,1]{1,0:T(8,128)S(1)} %slice.63), channel_id=1, source_target_pairs={{0,1},{2,3},{4,5},{6,7},{8,9},{10,11},{12,13},{14,15},{16,17},{18,... | collective-permute-start | bytes 200 | tf_op jit(solution)/shard_map/ppermute | solution.py:18
  7.3 16.1 %collective-permute-start.4 = (f32[1,2,40,16,128]{4,2,3,1,0:T(8,128)S(1)}, f32[1,2,40,16,128]{4,2,3,1,0:T(8,128)S(1)}, u32[]{:S(2)}, u32[]{:S(2)}) collective-permute-start(f32[1,2,40,16,128]{4,2,3,1,0:T(8,128)S(1)} %copy_multiply_fusion), channel_id=1, source_target_pairs={{0,16},{16,0},{1,17},{17,1},{2,18},{18,2},{3,19},{19,3},{4,20},{20... | collective-permute-start | bytes 1966088 | tf_op jit(solution)/shard_map/ppermute | solution.py:57
  26.1 6.7 %collective-permute-start = (f32[1,2,40,1,128]{4,2,3,1,0:T(8,128)S(1)}, f32[1,2,40,1,128]{4,2,3,1,0:T(8,128)S(1)}, u32[]{:S(2)}, u32[]{:S(2)}) collective-permute-start(f32[1,2,40,1,128]{4,2,3,1,0:T(8,128)S(1)} %get-tuple-element.102), channel_id=1, source_target_pairs={{0,2},{2,4},{4,6},{6,8},{8,10},{10,12},{12,14},{14,0},{1,3},{3,5},... | collective-permute-start | bytes 122888 | tf_op jit(solution)/shard_map/while/body/eval_jaxpr/ppermute | solution.py:28
  27.6 5.2 %collective-permute-start.1 = (f32[1,2,40,1,128]{4,2,3,1,0:T(8,128)S(1)}, f32[1,2,40,1,128]{4,2,3,1,0:T(8,128)S(1)}, u32[]{:S(2)}, u32[]{:S(2)}) collective-permute-start(f32[1,2,40,1,128]{4,2,3,1,0:T(8,128)S(1)} %get-tuple-element.103), channel_id=1, source_target_pairs={{2,0},{4,2},{6,4},{8,6},{10,8},{12,10},{14,12},{0,14},{3,1},{5,3},... | collective-permute-start | bytes 122888 | tf_op jit(solution)/shard_map/while/body/eval_jaxpr/ppermute | solution.py:30
  33.7 1.8 %collective-permute-start.3 = (f32[1,2,40,18,1]{2,1,4,3,0:T(2,128)S(1)}, f32[1,2,40,18,1]{2,1,4,3,0:T(2,128)S(1)}, u32[]{:S(2)}, u32[]{:S(2)}) collective-permute-start(f32[1,2,40,18,1]{2,1,4,3,0:T(2,128)S(1)} %copy.35), channel_id=1, source_target_pairs={{1,0},{0,1},{3,2},{2,3},{5,4},{4,5},{7,6},{6,7},{9,8},{8,9},{11,10... | collective-permute-start | bytes 17288 | tf_op jit(solution)/shard_map/while/body/eval_jaxpr/ppermute | solution.py:30
  38.4 6.7 %collective-permute-start = (f32[1,2,40,1,128]{4,2,3,1,0:T(8,128)S(1)}, f32[1,2,40,1,128]{4,2,3,1,0:T(8,128)S(1)}, u32[]{:S(2)}, u32[]{:S(2)}) collective-permute-start(f32[1,2,40,1,128]{4,2,3,1,0:T(8,128)S(1)} %get-tuple-element.102), channel_id=1, source_target_pairs={{0,2},{2,4},{4,6},{6,8},{8,10},{10,12},{12,14},{14,0},{1,3},{3,5},... | collective-permute-start | bytes 122888 | tf_op jit(solution)/shard_map/while/body/eval_jaxpr/ppermute | solution.py:28
  39.5 5.6 %collective-permute-start.1 = (f32[1,2,40,1,128]{4,2,3,1,0:T(8,128)S(1)}, f32[1,2,40,1,128]{4,2,3,1,0:T(8,128)S(1)}, u32[]{:S(2)}, u32[]{:S(2)}) collective-permute-start(f32[1,2,40,1,128]{4,2,3,1,0:T(8,128)S(1)} %get-tuple-element.103), channel_id=1, source_target_pairs={{2,0},{4,2},{6,4},{8,6},{10,8},{12,10},{14,12},{0,14},{3,1},{5,3},... | collective-permute-start | bytes 122888 | tf_op jit(solution)/shard_map/while/body/eval_jaxpr/ppermute | solution.py:30
  46.0 1.8 %collective-permute-start.3 = (f32[1,2,40,18,1]{2,1,4,3,0:T(2,128)S(1)}, f32[1,2,40,18,1]{2,1,4,3,0:T(2,128)S(1)}, u32[]{:S(2)}, u32[]{:S(2)}) collective-permute-start(f32[1,2,40,18,1]{2,1,4,3,0:T(2,128)S(1)} %copy.35), channel_id=1, source_target_pairs={{1,0},{0,1},{3,2},{2,3},{5,4},{4,5},{7,6},{6,7},{9,8},{8,9},{11,10... | collective-permute-start | bytes 17288 | tf_op jit(solution)/shard_map/while/body/eval_jaxpr/ppermute | solution.py:30
  50.6 6.7 %collective-permute-start = (f32[1,2,40,1,128]{4,2,3,1,0:T(8,128)S(1)}, f32[1,2,40,1,128]{4,2,3,1,0:T(8,128)S(1)}, u32[]{:S(2)}, u32[]{:S(2)}) collective-permute-start(f32[1,2,40,1,128]{4,2,3,1,0:T(8,128)S(1)} %get-tuple-element.102), channel_id=1, source_target_pairs={{0,2},{2,4},{4,6},{6,8},{8,10},{10,12},{12,14},{14,0},{1,3},{3,5},... | collective-permute-start | bytes 122888 | tf_op jit(solution)/shard_map/while/body/eval_jaxpr/ppermute | solution.py:28
  50.7 6.7 %collective-permute-start.1 = (f32[1,2,40,1,128]{4,2,3,1,0:T(8,128)S(1)}, f32[1,2,40,1,128]{4,2,3,1,0:T(8,128)S(1)}, u32[]{:S(2)}, u32[]{:S(2)}) collective-permute-start(f32[1,2,40,1,128]{4,2,3,1,0:T(8,128)S(1)} %get-tuple-element.103), channel_id=1, source_target_pairs={{2,0},{4,2},{6,4},{8,6},{10,8},{12,10},{14,12},{0,14},{3,1},{5,3},... | collective-permute-start | bytes 122888 | tf_op jit(solution)/shard_map/while/body/eval_jaxpr/ppermute | solution.py:30
  58.3 1.8 %collective-permute-start.3 = (f32[1,2,40,18,1]{2,1,4,3,0:T(2,128)S(1)}, f32[1,2,40,18,1]{2,1,4,3,0:T(2,128)S(1)}, u32[]{:S(2)}, u32[]{:S(2)}) collective-permute-start(f32[1,2,40,18,1]{2,1,4,3,0:T(2,128)S(1)} %copy.35), channel_id=1, source_target_pairs={{1,0},{0,1},{3,2},{2,3},{5,4},{4,5},{7,6},{6,7},{9,8},{8,9},{11,10... | collective-permute-start | bytes 17288 | tf_op jit(solution)/shard_map/while/body/eval_jaxpr/ppermute | solution.py:30
  62.9 6.7 %collective-permute-start = (f32[1,2,40,1,128]{4,2,3,1,0:T(8,128)S(1)}, f32[1,2,40,1,128]{4,2,3,1,0:T(8,128)S(1)}, u32[]{:S(2)}, u32[]{:S(2)}) collective-permute-start(f32[1,2,40,1,128]{4,2,3,1,0:T(8,128)S(1)} %get-tuple-element.102), channel_id=1, source_target_pairs={{0,2},{2,4},{4,6},{6,8},{8,10},{10,12},{12,14},{14,0},{1,3},{3,5},... | collective-permute-start | bytes 122888 | tf_op jit(solution)/shard_map/while/body/eval_jaxpr/ppermute | solution.py:28
  62.9 6.8 %collective-permute-start.1 = (f32[1,2,40,1,128]{4,2,3,1,0:T(8,128)S(1)}, f32[1,2,40,1,128]{4,2,3,1,0:T(8,128)S(1)}, u32[]{:S(2)}, u32[]{:S(2)}) collective-permute-start(f32[1,2,40,1,128]{4,2,3,1,0:T(8,128)S(1)} %get-tuple-element.103), channel_id=1, source_target_pairs={{2,0},{4,2},{6,4},{8,6},{10,8},{12,10},{14,12},{0,14},{3,1},{5,3},... | collective-permute-start | bytes 122888 | tf_op jit(solution)/shard_map/while/body/eval_jaxpr/ppermute | solution.py:30
  70.6 1.8 %collective-permute-start.3 = (f32[1,2,40,18,1]{2,1,4,3,0:T(2,128)S(1)}, f32[1,2,40,18,1]{2,1,4,3,0:T(2,128)S(1)}, u32[]{:S(2)}, u32[]{:S(2)}) collective-permute-start(f32[1,2,40,18,1]{2,1,4,3,0:T(2,128)S(1)} %copy.35), channel_id=1, source_target_pairs={{1,0},{0,1},{3,2},{2,3},{5,4},{4,5},{7,6},{6,7},{9,8},{8,9},{11,10... | collective-permute-start | bytes 17288 | tf_op jit(solution)/shard_map/while/body/eval_jaxpr/ppermute | solution.py:30
  75.2 6.7 %collective-permute-start = (f32[1,2,40,1,128]{4,2,3,1,0:T(8,128)S(1)}, f32[1,2,40,1,128]{4,2,3,1,0:T(8,128)S(1)}, u32[]{:S(2)}, u32[]{:S(2)}) collective-permute-start(f32[1,2,40,1,128]{4,2,3,1,0:T(8,128)S(1)} %get-tuple-element.102), channel_id=1, source_target_pairs={{0,2},{2,4},{4,6},{6,8},{8,10},{10,12},{12,14},{14,0},{1,3},{3,5},... | collective-permute-start | bytes 122888 | tf_op jit(solution)/shard_map/while/body/eval_jaxpr/ppermute | solution.py:28
  75.2 6.7 %collective-permute-start.1 = (f32[1,2,40,1,128]{4,2,3,1,0:T(8,128)S(1)}, f32[1,2,40,1,128]{4,2,3,1,0:T(8,128)S(1)}, u32[]{:S(2)}, u32[]{:S(2)}) collective-permute-start(f32[1,2,40,1,128]{4,2,3,1,0:T(8,128)S(1)} %get-tuple-element.103), channel_id=1, source_target_pairs={{2,0},{4,2},{6,4},{8,6},{10,8},{12,10},{14,12},{0,14},{3,1},{5,3},... | collective-permute-start | bytes 122888 | tf_op jit(solution)/shard_map/while/body/eval_jaxpr/ppermute | solution.py:30
  82.9 1.8 %collective-permute-start.3 = (f32[1,2,40,18,1]{2,1,4,3,0:T(2,128)S(1)}, f32[1,2,40,18,1]{2,1,4,3,0:T(2,128)S(1)}, u32[]{:S(2)}, u32[]{:S(2)}) collective-permute-start(f32[1,2,40,18,1]{2,1,4,3,0:T(2,128)S(1)} %copy.35), channel_id=1, source_target_pairs={{1,0},{0,1},{3,2},{2,3},{5,4},{4,5},{7,6},{6,7},{9,8},{8,9},{11,10... | collective-permute-start | bytes 17288 | tf_op jit(solution)/shard_map/while/body/eval_jaxpr/ppermute | solution.py:30
  87.5 6.7 %collective-permute-start = (f32[1,2,40,1,128]{4,2,3,1,0:T(8,128)S(1)}, f32[1,2,40,1,128]{4,2,3,1,0:T(8,128)S(1)}, u32[]{:S(2)}, u32[]{:S(2)}) collective-permute-start(f32[1,2,40,1,128]{4,2,3,1,0:T(8,128)S(1)} %get-tuple-element.102), channel_id=1, source_target_pairs={{0,2},{2,4},{4,6},{6,8},{8,10},{10,12},{12,14},{14,0},{1,3},{3,5},... | collective-permute-start | bytes 122888 | tf_op jit(solution)/shard_map/while/body/eval_jaxpr/ppermute | solution.py:28
  87.5 6.8 %collective-permute-start.1 = (f32[1,2,40,1,128]{4,2,3,1,0:T(8,128)S(1)}, f32[1,2,40,1,128]{4,2,3,1,0:T(8,128)S(1)}, u32[]{:S(2)}, u32[]{:S(2)}) collective-permute-start(f32[1,2,40,1,128]{4,2,3,1,0:T(8,128)S(1)} %get-tuple-element.103), channel_id=1, source_target_pairs={{2,0},{4,2},{6,4},{8,6},{10,8},{12,10},{14,12},{0,14},{3,1},{5,3},... | collective-permute-start | bytes 122888 | tf_op jit(solution)/shard_map/while/body/eval_jaxpr/ppermute | solution.py:30
  95.2 1.8 %collective-permute-start.3 = (f32[1,2,40,18,1]{2,1,4,3,0:T(2,128)S(1)}, f32[1,2,40,18,1]{2,1,4,3,0:T(2,128)S(1)}, u32[]{:S(2)}, u32[]{:S(2)}) collective-permute-start(f32[1,2,40,18,1]{2,1,4,3,0:T(2,128)S(1)} %copy.35), channel_id=1, source_target_pairs={{1,0},{0,1},{3,2},{2,3},{5,4},{4,5},{7,6},{6,7},{9,8},{8,9},{11,10... | collective-permute-start | bytes 17288 | tf_op jit(solution)/shard_map/while/body/eval_jaxpr/ppermute | solution.py:30
  99.8 6.7 %collective-permute-start = (f32[1,2,40,1,128]{4,2,3,1,0:T(8,128)S(1)}, f32[1,2,40,1,128]{4,2,3,1,0:T(8,128)S(1)}, u32[]{:S(2)}, u32[]{:S(2)}) collective-permute-start(f32[1,2,40,1,128]{4,2,3,1,0:T(8,128)S(1)} %get-tuple-element.102), channel_id=1, source_target_pairs={{0,2},{2,4},{4,6},{6,8},{8,10},{10,12},{12,14},{14,0},{1,3},{3,5},... | collective-permute-start | bytes 122888 | tf_op jit(solution)/shard_map/while/body/eval_jaxpr/ppermute | solution.py:28
  99.8 6.7 %collective-permute-start.1 = (f32[1,2,40,1,128]{4,2,3,1,0:T(8,128)S(1)}, f32[1,2,40,1,128]{4,2,3,1,0:T(8,128)S(1)}, u32[]{:S(2)}, u32[]{:S(2)}) collective-permute-start(f32[1,2,40,1,128]{4,2,3,1,0:T(8,128)S(1)} %get-tuple-element.103), channel_id=1, source_target_pairs={{2,0},{4,2},{6,4},{8,6},{10,8},{12,10},{14,12},{0,14},{3,1},{5,3},... | collective-permute-start | bytes 122888 | tf_op jit(solution)/shard_map/while/body/eval_jaxpr/ppermute | solution.py:30
  107.4 1.8 %collective-permute-start.3 = (f32[1,2,40,18,1]{2,1,4,3,0:T(2,128)S(1)}, f32[1,2,40,18,1]{2,1,4,3,0:T(2,128)S(1)}, u32[]{:S(2)}, u32[]{:S(2)}) collective-permute-start(f32[1,2,40,18,1]{2,1,4,3,0:T(2,128)S(1)} %copy.35), channel_id=1, source_target_pairs={{1,0},{0,1},{3,2},{2,3},{5,4},{4,5},{7,6},{6,7},{9,8},{8,9},{11,10... | collective-permute-start | bytes 17288 | tf_op jit(solution)/shard_map/while/body/eval_jaxpr/ppermute | solution.py:30
  112.1 6.7 %collective-permute-start = (f32[1,2,40,1,128]{4,2,3,1,0:T(8,128)S(1)}, f32[1,2,40,1,128]{4,2,3,1,0:T(8,128)S(1)}, u32[]{:S(2)}, u32[]{:S(2)}) collective-permute-start(f32[1,2,40,1,128]{4,2,3,1,0:T(8,128)S(1)} %get-tuple-element.102), channel_id=1, source_target_pairs={{0,2},{2,4},{4,6},{6,8},{8,10},{10,12},{12,14},{14,0},{1,3},{3,5},... | collective-permute-start | bytes 122888 | tf_op jit(solution)/shard_map/while/body/eval_jaxpr/ppermute | solution.py:28
  112.1 6.8 %collective-permute-start.1 = (f32[1,2,40,1,128]{4,2,3,1,0:T(8,128)S(1)}, f32[1,2,40,1,128]{4,2,3,1,0:T(8,128)S(1)}, u32[]{:S(2)}, u32[]{:S(2)}) collective-permute-start(f32[1,2,40,1,128]{4,2,3,1,0:T(8,128)S(1)} %get-tuple-element.103), channel_id=1, source_target_pairs={{2,0},{4,2},{6,4},{8,6},{10,8},{12,10},{14,12},{0,14},{3,1},{5,3},... | collective-permute-start | bytes 122888 | tf_op jit(solution)/shard_map/while/body/eval_jaxpr/ppermute | solution.py:30
  119.7 1.8 %collective-permute-start.3 = (f32[1,2,40,18,1]{2,1,4,3,0:T(2,128)S(1)}, f32[1,2,40,18,1]{2,1,4,3,0:T(2,128)S(1)}, u32[]{:S(2)}, u32[]{:S(2)}) collective-permute-start(f32[1,2,40,18,1]{2,1,4,3,0:T(2,128)S(1)} %copy.35), channel_id=1, source_target_pairs={{1,0},{0,1},{3,2},{2,3},{5,4},{4,5},{7,6},{6,7},{9,8},{8,9},{11,10... | collective-permute-start | bytes 17288 | tf_op jit(solution)/shard_map/while/body/eval_jaxpr/ppermute | solution.py:30
  124.4 6.7 %collective-permute-start = (f32[1,2,40,1,128]{4,2,3,1,0:T(8,128)S(1)}, f32[1,2,40,1,128]{4,2,3,1,0:T(8,128)S(1)}, u32[]{:S(2)}, u32[]{:S(2)}) collective-permute-start(f32[1,2,40,1,128]{4,2,3,1,0:T(8,128)S(1)} %get-tuple-element.102), channel_id=1, source_target_pairs={{0,2},{2,4},{4,6},{6,8},{8,10},{10,12},{12,14},{14,0},{1,3},{3,5},... | collective-permute-start | bytes 122888 | tf_op jit(solution)/shard_map/while/body/eval_jaxpr/ppermute | solution.py:28
  124.4 6.7 %collective-permute-start.1 = (f32[1,2,40,1,128]{4,2,3,1,0:T(8,128)S(1)}, f32[1,2,40,1,128]{4,2,3,1,0:T(8,128)S(1)}, u32[]{:S(2)}, u32[]{:S(2)}) collective-permute-start(f32[1,2,40,1,128]{4,2,3,1,0:T(8,128)S(1)} %get-tuple-element.103), channel_id=1, source_target_pairs={{2,0},{4,2},{6,4},{8,6},{10,8},{12,10},{14,12},{0,14},{3,1},{5,3},... | collective-permute-start | bytes 122888 | tf_op jit(solution)/shard_map/while/body/eval_jaxpr/ppermute | solution.py:30
  132.0 1.8 %collective-permute-start.3 = (f32[1,2,40,18,1]{2,1,4,3,0:T(2,128)S(1)}, f32[1,2,40,18,1]{2,1,4,3,0:T(2,128)S(1)}, u32[]{:S(2)}, u32[]{:S(2)}) collective-permute-start(f32[1,2,40,18,1]{2,1,4,3,0:T(2,128)S(1)} %copy.35), channel_id=1, source_target_pairs={{1,0},{0,1},{3,2},{2,3},{5,4},{4,5},{7,6},{6,7},{9,8},{8,9},{11,10... | collective-permute-start | bytes 17288 | tf_op jit(solution)/shard_map/while/body/eval_jaxpr/ppermute | solution.py:30
  136.6 6.7 %collective-permute-start = (f32[1,2,40,1,128]{4,2,3,1,0:T(8,128)S(1)}, f32[1,2,40,1,128]{4,2,3,1,0:T(8,128)S(1)}, u32[]{:S(2)}, u32[]{:S(2)}) collective-permute-start(f32[1,2,40,1,128]{4,2,3,1,0:T(8,128)S(1)} %get-tuple-element.102), channel_id=1, source_target_pairs={{0,2},{2,4},{4,6},{6,8},{8,10},{10,12},{12,14},{14,0},{1,3},{3,5},... | collective-permute-start | bytes 122888 | tf_op jit(solution)/shard_map/while/body/eval_jaxpr/ppermute | solution.py:28
  136.7 6.8 %collective-permute-start.1 = (f32[1,2,40,1,128]{4,2,3,1,0:T(8,128)S(1)}, f32[1,2,40,1,128]{4,2,3,1,0:T(8,128)S(1)}, u32[]{:S(2)}, u32[]{:S(2)}) collective-permute-start(f32[1,2,40,1,128]{4,2,3,1,0:T(8,128)S(1)} %get-tuple-element.103), channel_id=1, source_target_pairs={{2,0},{4,2},{6,4},{8,6},{10,8},{12,10},{14,12},{0,14},{3,1},{5,3},... | collective-permute-start | bytes 122888 | tf_op jit(solution)/shard_map/while/body/eval_jaxpr/ppermute | solution.py:30
  (14 other events, 32.0 us)
